TPU v7x, 256 devices: a whole 4x4x8 slice. The times are simulated.
256 devices in a mesh: blk: 256 (over y, z, x, core).
Axes of the slice: x: 4, y: 4, z: 8, core: 2. Of those that a mesh axis runs over, the one named last changes fastest.
Arguments:
- image: bfloat16 [131072, 1152], P('blk'), may hold values from -2 to 2
- text: bfloat16 [131072, 1152], P('blk'), may hold values from -2 to 2
- scale: float32 [1], replicated, may hold values from 4 to 16
- bias: float32 [1], replicated, may hold values from -4 to -1
Outputs:
- grad_image: float32 [131072, 1152], P('blk')
- grad_text: float32 [131072, 1152], P('blk')
All inputs are finite; a program needn't handle non-finite values.
Results may differ from a plain program's by a relative error of at most 0.0046.
Values may be sent and summed in bfloat16 or wider, within the bound.
A program may use at most 64 MiB of HBM per device.

v0:
```python
import jax
import jax.numpy as jnp
from jax import lax
from jax.sharding import PartitionSpec as P

STEPS = 4


def shifted(x, axis, by):
    peers = lax.axis_size(axis)
    return lax.ppermute(x, axis, [(i, (i + by) % peers) for i in range(peers)])


def normalize(values):
    wide = values.astype(jnp.float32)
    norms = jnp.sqrt(jnp.sum(wide * wide, axis=-1, keepdims=True) + 1e-06)
    return (wide / norms, norms)


def norm_back(grad_unit, unit, norms):
    inner = jnp.sum(unit * grad_unit, axis=-1, keepdims=True)
    return (grad_unit - unit * inner) / norms


def tile_weights(images, texts, factor, offset, diagonal):
    logits = (
        factor
        * lax.dot_general(
            images, texts, (((1,), (1,)), ((), ())), preferred_element_type=jnp.float32
        )
        + offset
    )
    probs = jax.nn.sigmoid(logits)
    if diagonal:
        count = images.shape[0]
        probs = probs - (jnp.arange(count)[:, None] == jnp.arange(count)[None, :]).astype(
            jnp.float32
        )
    return (factor * probs).astype(jnp.bfloat16)


def image_term(weights, texts):
    return jnp.dot(weights, texts, preferred_element_type=jnp.float32)


def text_term(weights, images):
    return lax.dot_general(
        weights, images, (((0,), (0,)), ((), ())), preferred_element_type=jnp.float32
    )


def next_texts(texts):
    return shifted(texts, "blk", 1)


def local(image, text, scale, bias):
    factor = scale[0]
    offset = bias[0]
    unit_image, image_norm = normalize(image)
    unit_text, text_norm = normalize(text)
    image_low = unit_image.astype(jnp.bfloat16)
    text_low = unit_text.astype(jnp.bfloat16)
    first = tile_weights(image_low, text_low, factor, offset, True)
    grad_unit_image = image_term(first, text_low)
    grad_unit_text = text_term(first, image_low)
    texts_here = text_low
    carried = grad_unit_text
    for step in range(1, STEPS):
        texts_here = next_texts(texts_here)
        carried = shifted(carried, "blk", 1)
        weights = tile_weights(image_low, texts_here, factor, offset, False)
        grad_unit_image = grad_unit_image + image_term(weights, texts_here)
        carried = carried + text_term(weights, image_low)
    grad_unit_text = shifted(carried, "blk", 1 - STEPS)
    grad_image = norm_back(grad_unit_image, unit_image, image_norm)
    grad_text = norm_back(grad_unit_text, unit_text, text_norm)
    return (grad_image, grad_text)


def solution(mesh):
    in_specs = (P("blk", None), P("blk", None), P(), P())
    out_specs = (P("blk", None), P("blk", None))
    return jax.shard_map(local, mesh=mesh, in_specs=in_specs, out_specs=out_specs, check_vma=False)
```

profile of v0, /device:TPU:0, one launch (start us, length us, event | category | flops | bytes accessed | tf_op | source)
XLA Modules:
  0.0 205.8 jit_solution(9792367636029390142)
XLA Ops:
  0.6 1.7 fusion
  2.3 1.6 fusion.31
  4.0 0.3 fusion.1
  4.3 0.4 fusion.32
  6.0 1.0 fusion.27
  7.0 0.9 fusion.34
  8.1 47.3 %collective-permute-done = bf16[512,1152]{1,0:T(8,128)(2,1)S(1)} collective-permute-done((bf16[512,1152]{1,0:T(8,128)(2,1)S(1)}, bf16[512,1152]{1,0:T(8,128)(2,1)S(1)}, u32[]{:S(2)}, u32[]{:S(2)}) %collective-permute-start) | collective-permute-done | bytes 1179680 | tf_op jit(solution)/shard_map/ppermute | solution.py:11
  55.3 1.0 fusion.30
  56.4 0.9 convolution_add_fusion
  57.4 46.2 %collective-permute-done.1 = bf16[512,1152]{1,0:T(8,128)(2,1)S(1)} collective-permute-done((bf16[512,1152]{1,0:T(8,128)(2,1)S(1)}, bf16[512,1152]{1,0:T(8,128)(2,1)S(1)}, u32[]{:S(2)}, u32[]{:S(2)}) %collective-permute-start.1) | collective-permute-done | bytes 1179680 | tf_op jit(solution)/shard_map/ppermute | solution.py:11
  103.7 1.0 fusion.29
  104.7 0.9 fusion.35
  106.2 52.8 %collective-permute-done.2 = bf16[512,1152]{1,0:T(8,128)(2,1)S(1)} collective-permute-done((bf16[512,1152]{1,0:T(8,128)(2,1)S(1)}, bf16[512,1152]{1,0:T(8,128)(2,1)S(1)}, u32[]{:S(2)}, u32[]{:S(2)}) %collective-permute-start.2) | collective-permute-done | bytes 1179680 | tf_op jit(solution)/shard_map/ppermute | solution.py:11
  159.0 1.0 fusion.28
  160.0 0.9 fusion.36
  161.2 0.8 fusion.33
  162.1 0.9 convolution_add_fusion.3
  163.0 0.9 convolution_add_fusion.2
  163.8 0.4 copy-done.1
  164.2 1.1 multiply_reduce_fusion.1
  165.4 1.9 subtract_divide_fusion.1
  167.3 36.2 %collective-permute-done.6 = f32[512,1152]{1,0:T(8,128)S(1)} collective-permute-done((f32[512,1152]{1,0:T(8,128)S(1)}, f32[512,1152]{1,0:T(8,128)S(1)}, u32[]{:S(2)}, u32[]{:S(2)}) %collective-permute-start.6) | collective-permute-done | bytes 2359328 | tf_op jit(solution)/shard_map/ppermute | solution.py:11
  203.5 0.5 multiply_reduce_fusion
  203.9 1.9 subtract_divide_fusion
  (17 shorter events, 1.3 us)
Async XLA Ops:
  0.6 3.3 %copy-start = (bf16[512,1152]{1,0:T(8,128)(2,1)S(1)}, bf16[512,1152]{1,0:T(8,128)(2,1)}, u32[]{:S(2)}) copy-start(bf16[512,1152]{1,0:T(8,128)(2,1)} %param.5) | copy-start | bytes 3538948
  7.9 48.5 %collective-permute-start.3 = (f32[512,1152]{1,0:T(8,128)S(1)}, f32[512,1152]{1,0:T(8,128)S(1)}, u32[]{:S(2)}, u32[]{:S(2)}) collective-permute-start(f32[512,1152]{1,0:T(8,128)S(1)} %fusion.34), channel_id=1, source_target_pairs={{0,1},{1,2},{2,3},{3,4},{4,5},{5,6},{6,7},{7,8},{8,9},{9,10},{10,1... | collective-permute-start | bytes 7077896 | tf_op jit(solution)/shard_map/ppermute | solution.py:11
  8.0 47.4 %collective-permute-start = (bf16[512,1152]{1,0:T(8,128)(2,1)S(1)}, bf16[512,1152]{1,0:T(8,128)(2,1)S(1)}, u32[]{:S(2)}, u32[]{:S(2)}) collective-permute-start(bf16[512,1152]{1,0:T(8,128)(2,1)S(1)} %fusion.32), channel_id=1, source_target_pairs={{0,1},{1,2},{2,3},{3,4},{4,5},{5,6},{6,7},{7,8},{8,9},{9,10},{10,1... | collective-permute-start | bytes 3538952 | tf_op jit(solution)/shard_map/ppermute | solution.py:11
  57.3 48.3 %collective-permute-start.4 = (f32[512,1152]{1,0:T(8,128)S(1)}, f32[512,1152]{1,0:T(8,128)S(1)}, u32[]{:S(2)}, u32[]{:S(2)}) collective-permute-start(f32[512,1152]{1,0:T(8,128)S(1)} %convolution_add_fusion), channel_id=1, source_target_pairs={{0,1},{1,2},{2,3},{3,4},{4,5},{5,6},{6,7},{7,8},{8,9},{9,10},{10,1... | collective-permute-start | bytes 7077896 | tf_op jit(solution)/shard_map/ppermute | solution.py:11
  57.3 46.3 %collective-permute-start.1 = (bf16[512,1152]{1,0:T(8,128)(2,1)S(1)}, bf16[512,1152]{1,0:T(8,128)(2,1)S(1)}, u32[]{:S(2)}, u32[]{:S(2)}) collective-permute-start(bf16[512,1152]{1,0:T(8,128)(2,1)S(1)} %collective-permute-done), channel_id=1, source_target_pairs={{0,1},{1,2},{2,3},{3,4},{4,5},{5,6},{6,7},{7,8},{8,9},{9,10},{10,1... | collective-permute-start | bytes 3538952 | tf_op jit(solution)/shard_map/ppermute | solution.py:11
  105.8 55.1 %collective-permute-start.5 = (f32[512,1152]{1,0:T(8,128)S(1)}, f32[512,1152]{1,0:T(8,128)S(1)}, u32[]{:S(2)}, u32[]{:S(2)}) collective-permute-start(f32[512,1152]{1,0:T(8,128)S(1)} %add.79), channel_id=1, source_target_pairs={{0,1},{1,2},{2,3},{3,4},{4,5},{5,6},{6,7},{7,8},{8,9},{9,10},{10,1... | collective-permute-start | bytes 7077896 | tf_op jit(solution)/shard_map/ppermute | solution.py:11
  105.9 53.1 %collective-permute-start.2 = (bf16[512,1152]{1,0:T(8,128)(2,1)S(1)}, bf16[512,1152]{1,0:T(8,128)(2,1)S(1)}, u32[]{:S(2)}, u32[]{:S(2)}) collective-permute-start(bf16[512,1152]{1,0:T(8,128)(2,1)S(1)} %collective-permute-done.1), channel_id=1, source_target_pairs={{0,1},{1,2},{2,3},{3,4},{4,5},{5,6},{6,7},{7,8},{8,9},{9,10},{10,1... | collective-permute-start | bytes 3538952 | tf_op jit(solution)/shard_map/ppermute | solution.py:11
  161.2 42.3 %collective-permute-start.6 = (f32[512,1152]{1,0:T(8,128)S(1)}, f32[512,1152]{1,0:T(8,128)S(1)}, u32[]{:S(2)}, u32[]{:S(2)}) collective-permute-start(f32[512,1152]{1,0:T(8,128)S(1)} %add.80), channel_id=1, source_target_pairs={{0,253},{1,254},{2,255},{3,0},{4,1},{5,2},{6,3},{7,4},{8,5},{9,6},... | collective-permute-start | bytes 7077896 | tf_op jit(solution)/shard_map/ppermute | solution.py:11
  163.0 1.3 copy-start.1
where the time goes:
time: 206 us
  waiting for transfers between devices  183 us (89%)
  matrix products  11.3 us (5%)
  other arithmetic  8.72 us (4%)
  between operations  2.13 us (1%)
    ppermute x7, waiting for transfers between devices, shifted(): return lax.ppermute(x, axis, [(i, (i + by) % peers) for i in range(peers)])  183 us
  transfers between devices with their start and end apart: 7, of which 4 were waited for; matrix products, arithmetic and copies ran while one was open for 5% of the time, Pallas kernels for 0%

commit v1 on v0

v1 whole, which is shorter than its diff:
```python
import functools

import jax
import jax.numpy as jnp
from jax import lax
from jax.experimental import pallas as pl
from jax.experimental.pallas import tpu as pltpu
from jax.sharding import PartitionSpec as P

MESH = pl.DeviceIdType.MESH
CHUNK = 128
TILE = 256
EPS = 1e-06


def inverse_norm(wide):
    return lax.rsqrt(jnp.sum(wide * wide, axis=-1, keepdims=True) + EPS)


def exchange(n, scale_ref, bias_ref, image_ref, text_ref, out_ref, x_raw, y_raw, x_low, y_low, x_sum, y_sum,
             passed, near, far, unit, load_sem, link_send, link_recv, pass_send, pass_recv, pair_send, pair_recv):
    rows, _ = x_raw.shape
    parts = rows // CHUNK
    me = lax.axis_index("blk")
    core = lax.rem(me, 2)
    partner = me + 1 - 2 * core
    ahead = lax.rem(me + 2 - 4 * core + n, n)
    behind = lax.rem(me - 2 + 4 * core + n, n)
    factor = scale_ref[0]
    offset = bias_ref[0]

    def load(x_ref, y_ref):
        pltpu.make_async_copy(y_ref, y_raw, load_sem.at[0]).start()
        pltpu.make_async_copy(x_ref, x_raw, load_sem.at[1]).start()

    pl.when(core == 0)(lambda: load(image_ref, text_ref))
    pl.when(core == 1)(lambda: load(text_ref, image_ref))

    barrier = pltpu.get_barrier_semaphore()
    for other in (partner, ahead, behind):
        pl.semaphore_signal(barrier, inc=1, device_id=(other,), device_id_type=MESH)
    pl.semaphore_wait(barrier, 3)

    def part(i):
        return pl.ds(pl.multiple_of(i * CHUNK, CHUNK), CHUNK)

    def link(src, i):
        return pltpu.make_async_remote_copy(
            src_ref=src, dst_ref=far.at[part(i)], send_sem=link_send.at[i], recv_sem=link_recv.at[i],
            device_id=(ahead,), device_id_type=MESH)

    def hand(i):
        return pltpu.make_async_remote_copy(
            src_ref=x_raw.at[part(i)], dst_ref=passed.at[part(i)], send_sem=pass_send.at[i], recv_sem=pass_recv.at[i],
            device_id=(partner,), device_id_type=MESH)

    def pair(src, i):
        return pltpu.make_async_remote_copy(
            src_ref=src, dst_ref=near.at[part(i)], send_sem=pair_send.at[i], recv_sem=pair_recv.at[i],
            device_id=(partner,), device_id_type=MESH)

    pltpu.make_async_copy(text_ref, y_raw, load_sem.at[0]).wait()
    for i in range(parts):
        link(y_raw.at[part(i)], i).start()
    pltpu.make_async_copy(text_ref, x_raw, load_sem.at[1]).wait()
    for i in range(parts):
        hand(i).start()
    for i in range(parts):
        pair(y_raw.at[part(i)], i).start()

    def meet(anchor, chunk, total, diagonal=None):
        for t in range(rows // TILE):
            tile = pl.ds(t * TILE, TILE)
            logits = factor * lax.dot_general(
                anchor[tile, :], chunk, (((1,), (1,)), ((), ())), preferred_element_type=jnp.float32) + offset
            probs = jax.nn.sigmoid(logits)
            if diagonal is not None:
                row = lax.broadcasted_iota(jnp.int32, probs.shape, 0) + t * TILE
                column = lax.broadcasted_iota(jnp.int32, probs.shape, 1) + diagonal
                probs = probs - (row == column).astype(jnp.float32)
            weights = (factor * probs).astype(jnp.bfloat16)
            total[tile, :] += jnp.dot(weights, chunk, preferred_element_type=jnp.float32)

    def low(src):
        wide = src[...].astype(jnp.float32)
        return (wide * inverse_norm(wide)).astype(jnp.bfloat16)

    def meet_raw(anchor, src, total):
        unit[...] = low(src)
        meet(anchor, unit[...], total)

    @pl.loop(0, parts)
    def _(i):
        here = part(i)
        x_low[here, :] = low(x_raw.at[here])
        y_low[here, :] = low(y_raw.at[here])
        x_sum[here, :] = jnp.zeros((CHUNK, x_sum.shape[1]), jnp.float32)
        y_sum[here, :] = jnp.zeros((CHUNK, y_sum.shape[1]), jnp.float32)

    @pl.loop(0, parts)
    def _(i):
        here = part(i)
        meet(x_low, y_low[here, :], x_sum, i * CHUNK)
        meet(y_low, x_low[here, :], y_sum, i * CHUNK)
        pair(y_raw.at[here], i).wait_recv()
        meet_raw(y_low, near.at[here], y_sum)

    @pl.loop(0, parts)
    def _(i):
        link(y_raw.at[part(i)], i).wait_recv()
        pair(far.at[part(i)], i + parts).start()
        hand(i).wait_recv()
        link(passed.at[part(i)], i + parts).start()
        meet_raw(x_low, far.at[part(i)], x_sum)
        pair(far.at[part(i)], i + parts).wait_recv()
        meet_raw(y_low, near.at[part(i + parts)], y_sum)

    @pl.loop(0, parts)
    def _(i):
        j = i + parts
        link(y_raw.at[part(i)], j).wait_recv()
        pair(far.at[part(j)], j + parts).start()
        link(far.at[part(j)], j + parts).start()
        meet_raw(x_low, far.at[part(j)], x_sum)
        pair(far.at[part(j)], j + parts).wait_recv()
        meet_raw(y_low, near.at[part(j + parts)], y_sum)

    def finish(raw, total, which):
        @pl.loop(0, parts)
        def _(i):
            here = part(i)
            wide = raw[here, :].astype(jnp.float32)
            inverse = inverse_norm(wide)
            own = wide * inverse
            grad = total[here, :]
            inner = jnp.sum(own * grad, axis=-1, keepdims=True)
            out_ref[which, here, :] = (grad - own * inner) * inverse

    finish(y_raw, y_sum, 1 - core)

    @pl.loop(0, parts)
    def _(i):
        j = i + 2 * parts
        link(y_raw.at[part(i)], j).wait_recv()
        meet_raw(x_low, far.at[part(j)], x_sum)

    finish(x_raw, x_sum, core)

    @pl.loop(0, parts)
    def _(i):
        hand(i).wait_send()

    @pl.loop(0, 3 * parts)
    def _(i):
        link(y_raw.at[part(0)], i).wait_send()
        pair(y_raw.at[part(0)], i).wait_send()


def solution(mesh):
    n = mesh.shape["blk"]

    def local(image, text, scale, bias):
        rows, width = image.shape
        parts = rows // CHUNK
        dma = pltpu.SemaphoreType.DMA
        both = pl.pallas_call(
            functools.partial(exchange, n),
            out_shape=pltpu.VMEM((2, rows, width), jnp.float32),
            in_specs=[pl.BlockSpec(memory_space=pltpu.SMEM)] * 2 + [pl.BlockSpec(memory_space=pl.ANY)] * 2,
            out_specs=pl.BlockSpec(memory_space=pltpu.VMEM),
            scratch_shapes=[
                pltpu.VMEM((rows, width), jnp.bfloat16),
                pltpu.VMEM((rows, width), jnp.bfloat16),
                pltpu.VMEM((rows, width), jnp.bfloat16),
                pltpu.VMEM((rows, width), jnp.bfloat16),
                pltpu.VMEM((rows, width), jnp.float32),
                pltpu.VMEM((rows, width), jnp.float32),
                pltpu.VMEM((rows, width), jnp.bfloat16),
                pltpu.VMEM((3 * rows, width), jnp.bfloat16),
                pltpu.VMEM((3 * rows, width), jnp.bfloat16),
                pltpu.VMEM((CHUNK, width), jnp.bfloat16),
                dma((2,)),
                dma((3 * parts,)),
                dma((3 * parts,)),
                dma((parts,)),
                dma((parts,)),
                dma((3 * parts,)),
                dma((3 * parts,)),
            ],
            compiler_params=pltpu.CompilerParams(
                collective_id=0, has_side_effects=True, vmem_limit_bytes=40 * 2**20),
        )(scale, bias, image, text)
        return both[0], both[1]

    in_specs = (P("blk", None), P("blk", None), P(), P())
    out_specs = (P("blk", None), P("blk", None))
    return jax.shard_map(local, mesh=mesh, in_specs=in_specs, out_specs=out_specs, check_vma=False)
```

time: 206 us -> 62.5 us (0.30)
  the two profiles are of different devices: /device:TPU:0 before, /device:TPU:1 now
where the time goes in v1:
time: 62.5 us; the launch traced here: 62.4 us
  Pallas kernels  55.4 us (89%)
  local copies, waits for them, and re-layouts  5.02 us (8%)
  between operations  1.94 us (3%)
    pallas_call x1, Pallas kernels, local(): pl.pallas_call(functools.partial(exchange, n), out_shape=pltpu.VMEM((2, r...  55.4 us
    unnamed x4, local copies, waits for them, and re-layouts  2.53 us
    squeeze x1, local copies, waits for them, and re-layouts, local(): return (both[0], both[1])  2.49 us

profile of v1, /device:TPU:1, one launch (start us, length us, event | category | flops | bytes accessed | tf_op | source)
XLA Modules:
  0.0 62.4 jit_solution(18384199372462777361)
XLA Ops:
  1.9 0.0 copy-start
  1.9 1.3 %copy-done = bf16[512,1152]{1,0:T(8,128)(2,1)S(1)} copy-done((bf16[512,1152]{1,0:T(8,128)(2,1)S(1)}, bf16[512,1152]{1,0:T(8,128)(2,1)}, u32[]{:S(2)}) %copy-start) | copy-done | bytes 1179672
  3.2 0.0 copy-start.1
  3.2 1.3 %copy-done.1 = bf16[512,1152]{1,0:T(8,128)(2,1)S(1)} copy-done((bf16[512,1152]{1,0:T(8,128)(2,1)S(1)}, bf16[512,1152]{1,0:T(8,128)(2,1)}, u32[]{:S(2)}) %copy-start.1) | copy-done | bytes 1179672
  4.5 55.4 %shard_map.59 = f32[2,512,1152]{2,1,0:T(8,128)S(1)} custom-call(f32[1]{0:T(128)S(6)} %copy.6.scale_ref, f32[1]{0:T(128)S(6)} %copy.7.bias_ref, bf16[512,1152]{1,0:T(8,128)(2,1)S(1)} %copy-done, bf16[512,1152]{1,0:T(8,128)(2,1)S(1)} %copy-done.1), custom_call_target="tpu_custom_call" | custom-call | tf_op jit(solution)/shard_map/pallas_call | solution.py:166
  59.9 2.5 %slice_bitcast_fusion = (f32[512,1152]{1,0:T(8,128)}, f32[512,1152]{1,0:T(8,128)}) fusion(f32[2,512,1152]{2,1,0:T(8,128)S(1)} %shard_map.59), kind=kLoop, calls=%fused_computation | loop fusion | bytes 9437184 | tf_op jit(solution)/shard_map/squeeze | solution.py:193
Async XLA Ops:
  1.9 1.3 %copy-start = (bf16[512,1152]{1,0:T(8,128)(2,1)S(1)}, bf16[512,1152]{1,0:T(8,128)(2,1)}, u32[]{:S(2)}) copy-start(bf16[512,1152]{1,0:T(8,128)(2,1)} %image_ref.1) | copy-start | bytes 3538948
  3.2 1.3 %copy-start.1 = (bf16[512,1152]{1,0:T(8,128)(2,1)S(1)}, bf16[512,1152]{1,0:T(8,128)(2,1)}, u32[]{:S(2)}) copy-start(bf16[512,1152]{1,0:T(8,128)(2,1)} %text_ref.1) | copy-start | bytes 3538948

commit v2 on v0

v2 whole, which is shorter than its diff:
```python
import functools

import jax
import jax.numpy as jnp
from jax import lax
from jax.experimental import pallas as pl
from jax.experimental.pallas import tpu as pltpu
from jax.sharding import PartitionSpec as P

MESH = pl.DeviceIdType.MESH
CHUNK = 128
EPS = 1e-06
MEBI = 2**20


def inverse_norm(wide):
    return lax.rsqrt(jnp.sum(wide * wide, axis=-1, keepdims=True) + EPS)


def norm_back(raw, grad):
    wide = raw.astype(jnp.float32)
    inverse = inverse_norm(wide)
    own = wide * inverse
    inner = jnp.sum(own * grad, axis=-1, keepdims=True)
    return (grad - own * inner) * inverse


def weigh(anchor, others, factor, offset, diagonal=False):
    logits = factor * lax.dot_general(
        anchor, others, (((1,), (1,)), ((), ())), preferred_element_type=jnp.float32) + offset
    probs = jax.nn.sigmoid(logits)
    if diagonal:
        row = lax.broadcasted_iota(jnp.int32, probs.shape, 0)
        column = lax.broadcasted_iota(jnp.int32, probs.shape, 1)
        probs = probs - (row == column).astype(jnp.float32)
    return (factor * probs).astype(jnp.bfloat16)


def low(raw):
    wide = raw.astype(jnp.float32)
    return (wide * inverse_norm(wide)).astype(jnp.bfloat16)


def exchange(n, scale_ref, bias_ref, image_ref, text_ref, x_raw, x_low, x_sum, y_grad, last, y_raw, y_low, y_sum,
             passed, near, far, unit, load_sem, link_send, link_recv, pass_send, pass_recv, pair_send, pair_recv):
    rows, width = x_raw.shape
    parts = rows // CHUNK
    me = lax.axis_index("blk")
    core = lax.rem(me, 2)
    partner = me + 1 - 2 * core
    ahead = lax.rem(me + 2 - 4 * core + n, n)
    behind = lax.rem(me - 2 + 4 * core + n, n)

    barrier = pltpu.get_barrier_semaphore()
    for other in (behind, partner):
        pl.semaphore_signal(barrier, inc=1, device_id=(other,), device_id_type=MESH)

    def load(x_ref, y_ref):
        pltpu.make_async_copy(y_ref, y_raw, load_sem.at[0]).start()
        pltpu.make_async_copy(x_ref, x_raw, load_sem.at[1]).start()

    pl.when(core == 0)(lambda: load(image_ref, text_ref))
    pl.when(core == 1)(lambda: load(text_ref, image_ref))

    factor = scale_ref[0]
    offset = bias_ref[0]

    def part(i):
        return pl.ds(i * CHUNK, CHUNK)

    def remote(src, dst, send, recv, device):
        return pltpu.make_async_remote_copy(
            src_ref=src, dst_ref=dst, send_sem=send, recv_sem=recv, device_id=(device,), device_id_type=MESH)

    def link(src, i):
        return remote(src, far.at[part(i)], link_send.at[i], link_recv.at[i], ahead)

    def hand(i):
        return remote(x_raw.at[part(i)], passed.at[part(i)], pass_send.at[i], pass_recv.at[i], partner)

    def pair(src, i):
        return remote(src, near.at[part(i)], pair_send.at[i], pair_recv.at[i], partner)

    pltpu.make_async_copy(text_ref, y_raw, load_sem.at[0]).wait()
    pltpu.make_async_copy(text_ref, x_raw, load_sem.at[1]).wait()
    pl.semaphore_wait(barrier, 2)
    link(y_raw.at[part(0)], 0).start()
    for i in range(parts):
        hand(i).start()
    for i in range(parts):
        pair(y_raw.at[part(i)], i).start()

    def lower(src, start, dst, count):
        @pl.loop(0, count)
        def _(i):
            dst[pl.ds(pl.multiple_of(i * CHUNK, CHUNK), CHUNK), :] = low(
                src[pl.ds(pl.multiple_of(start + i * CHUNK, CHUNK), CHUNK), :])

    def meet(anchor, src, start, total, count=parts):
        lower(src, start, unit, count)
        others = unit[pl.ds(0, count * CHUNK), :]
        weights = weigh(anchor[...], others, factor, offset)
        total[...] += jnp.dot(weights, others, preferred_element_type=jnp.float32)

    lower(x_raw, 0, x_low, parts)
    for i in range(parts):
        hand(i).wait_recv()
        link(passed.at[part(i)], 1 + i).start()
    for i in range(1, parts):
        link(y_raw.at[part(i)], parts + i).start()
    lower(y_raw, 0, y_low, parts)

    x_sum[...] = jnp.dot(
        weigh(x_low[...], y_low[...], factor, offset, True), y_low[...], preferred_element_type=jnp.float32)
    y_sum[...] = jnp.dot(
        weigh(y_low[...], x_low[...], factor, offset, True), x_low[...], preferred_element_type=jnp.float32)
    for i in range(parts):
        pair(y_raw.at[part(i)], i).wait_recv()
    meet(y_low, near, 0, y_sum)

    for block in range(2):
        for i in range(block * parts, (block + 1) * parts):
            link(y_raw.at[part(0)], i).wait_recv()
            pair(far.at[part(i)], i + parts).start()
            if 1 <= i <= parts:
                link(far.at[part(i)], i + 2 * parts - 1).start()
        meet(x_low, far, block * rows, x_sum)
        for i in range(block * parts, (block + 1) * parts):
            pair(far.at[part(i)], i + parts).wait_recv()
        meet(y_low, near, (block + 1) * rows, y_sum)

    @pl.loop(0, parts)
    def _(i):
        here = pl.ds(pl.multiple_of(i * CHUNK, CHUNK), CHUNK)
        y_grad[here, :] = norm_back(y_raw[here, :], y_sum[here, :])

    for i in range(2 * parts, 3 * parts - 1):
        link(y_raw.at[part(0)], i).wait_recv()
    meet(x_low, far, 2 * rows, x_sum, parts - 1)

    for i in range(parts):
        hand(i).wait_send()
    for i in range(3 * parts):
        pair(y_raw.at[part(0)], i).wait_send()
    for i in range(3 * parts):
        link(y_raw.at[part(0)], i).wait_send()
    link(y_raw.at[part(0)], 3 * parts - 1).wait_recv()
    last[...] = low(far[part(3 * parts - 1), :])


def conclude(scale_ref, bias_ref, x_raw, x_low, x_sum, y_grad, last, image_out, text_out, x_grad, weights, store_sem):
    rows, _ = x_raw.shape
    parts = rows // CHUNK
    core = lax.rem(lax.axis_index("blk"), 2)

    def store(src, out, i):
        return pltpu.make_async_copy(src, out, store_sem.at[i])

    for i in range(parts):
        here = pl.ds(i * CHUNK, CHUNK)
        pl.when(core == 0)(lambda: store(y_grad.at[here], text_out.at[here], parts + i).start())
        pl.when(core == 1)(lambda: store(y_grad.at[here], image_out.at[here], parts + i).start())
    weights[...] = weigh(x_low[...], last[...], scale_ref[0], bias_ref[0])
    for i in range(parts):
        here = pl.ds(i * CHUNK, CHUNK)
        grad = x_sum[here, :] + jnp.dot(weights[here, :], last[...], preferred_element_type=jnp.float32)
        x_grad[here, :] = norm_back(x_raw[here, :], grad)
        pl.when(core == 0)(lambda: store(x_grad.at[here], image_out.at[here], i).start())
        pl.when(core == 1)(lambda: store(x_grad.at[here], text_out.at[here], i).start())
    for i in range(parts):
        here = pl.ds(i * CHUNK, CHUNK)
        store(x_grad.at[here], image_out.at[here], i).wait()
        store(y_grad.at[here], text_out.at[here], parts + i).wait()


def solution(mesh):
    n = mesh.shape["blk"]

    def local(image, text, scale, bias):
        rows, width = image.shape
        parts = rows // CHUNK
        dma = pltpu.SemaphoreType.DMA
        half = pltpu.VMEM((rows, width), jnp.bfloat16)
        wide = pltpu.VMEM((rows, width), jnp.float32)
        piece = pltpu.VMEM((CHUNK, width), jnp.bfloat16)
        in_hbm = pl.BlockSpec(memory_space=pltpu.HBM)
        in_vmem = pl.BlockSpec(memory_space=pltpu.VMEM)
        in_smem = pl.BlockSpec(memory_space=pltpu.SMEM)
        held = pl.pallas_call(
            functools.partial(exchange, n),
            out_shape=(half, half, wide, wide, piece),
            in_specs=[in_smem] * 2 + [in_hbm] * 2,
            out_specs=(in_vmem,) * 5,
            scratch_shapes=[
                half, half, wide, half,
                pltpu.VMEM((3 * rows, width), jnp.bfloat16),
                pltpu.VMEM((3 * rows, width), jnp.bfloat16),
                half,
                dma((2,)),
                dma((3 * parts,)),
                dma((3 * parts,)),
                dma((parts,)),
                dma((parts,)),
                dma((3 * parts,)),
                dma((3 * parts,)),
            ],
            compiler_params=pltpu.CompilerParams(
                collective_id=0, has_side_effects=True, vmem_limit_bytes=40 * MEBI),
        )(scale, bias, pltpu.with_memory_space_constraint(image, pltpu.HBM),
          pltpu.with_memory_space_constraint(text, pltpu.HBM))
        out = jax.ShapeDtypeStruct((rows, width), jnp.float32)
        return pl.pallas_call(
            conclude,
            out_shape=(out, out),
            in_specs=[in_smem] * 2 + [in_vmem] * 5,
            out_specs=(in_hbm,) * 2,
            scratch_shapes=[wide, pltpu.VMEM((rows, CHUNK), jnp.bfloat16), dma((2 * parts,))],
            compiler_params=pltpu.CompilerParams(vmem_limit_bytes=16 * MEBI),
        )(scale, bias, *held)

    in_specs = (P("blk", None), P("blk", None), P(), P())
    out_specs = (P("blk", None), P("blk", None))
    return jax.shard_map(local, mesh=mesh, in_specs=in_specs, out_specs=out_specs, check_vma=False)
```

time: 206 us -> 55.7 us (0.27)
  waiting for transfers between devices: 183 us -> 0 us
  Pallas kernels: 0 us -> 53.5 us
  matrix products: 11.3 us -> 0 us
  other arithmetic: 8.72 us -> 0 us
    ppermute x7 -> x0, waiting for transfers between devices: 183 us -> none  [shifted(): return lax.ppermute(x, axis, [(i, (i + by) % peers) for i in range(peers)])]
    pallas_call x0 -> x2, Pallas kernels: none -> 53.5 us  [the longest x1 50.7 us: local(): pl.pallas_call(functools.partial(exchange, n), out_shape=(half, half, wid...]
    dot_general x12 -> x0, matrix products: 11.3 us -> none  [the longest x4 4.1 us: tile_weights(): lax.dot_general(images, texts, (((1,), (1,)), ((), ())), preferred_elemen...]
    div x2 -> x0, other arithmetic: 3.78 us -> none  [norm_back(): return (grad_unit - unit * inner) / norms]
    reduce_sum x3 -> x0, other arithmetic: 2.44 us -> none  [the longest x2 1.98 us: normalize(): norms = jnp.sqrt(jnp.sum(wide * wide, axis=-1, keepdims=True) + 1e-06)]
  transfers between devices with their start and end apart: 7 -> 0, of which waited for: 4 -> 0; matrix products, arithmetic and copies ran while one was open for 5% -> 0% of each run, Pallas kernels for 0% -> 0%
where the time goes in v2:
time: 55.7 us; the launch traced here: 55.6 us
  Pallas kernels  53.5 us (96%)
  between operations  2.09 us (4%)
    pallas_call x1, Pallas kernels, local(): pl.pallas_call(functools.partial(exchange, n), out_shape=(half, half, wid...  50.7 us
    pallas_call x1, Pallas kernels, local(): pl.pallas_call(conclude, out_shape=(out, out), in_specs=[in_smem] * 2 + [...  2.82 us

profile of v2, /device:TPU:0, one launch (start us, length us, event | category | flops | bytes accessed | tf_op | source)
XLA Modules:
  0.0 55.6 jit_solution(18319800052690043826)
XLA Ops:
  1.9 50.7 %shard_map.59 = (bf16[512,1152]{1,0:T(8,128)(2,1)S(1)}, bf16[512,1152]{1,0:T(8,128)(2,1)S(1)}, f32[512,1152]{1,0:T(8,128)S(1)}, f32[512,1152]{1,0:T(8,128)S(1)}, bf16[128,1152]{1,0:T(8,128)(2,1)S(1)}) custom-call(f32[1]{0:T(128)S(6)} %copy.6.scale_ref, f32[1]{0:T(128)S(6)} %copy.7.bias_ref, bf16[512,1152]{1,0:T(8,128)(2,1)} %image_ref.1, ...), custom_call_target="tpu_custom_call" | custom-call | tf_op jit(solution)/shard_map/pallas_call | solution.py:189
  52.6 2.8 %shard_map.60 = (f32[512,1152]{1,0:T(8,128)}, f32[512,1152]{1,0:T(8,128)}) custom-call(f32[1]{0:T(128)S(6)} %copy.6.scale_ref, f32[1]{0:T(128)S(6)} %copy.7.bias_ref, bf16[512,1152]{1,0:T(8,128)(2,1)S(1)} %get-tuple-element.7.x_raw, bf16[512,1152]{1,0:T(8,128)(2,1)S(1)} %get-tuple-element.8.x_low, f32[512,1152]{1,0:T(8,128)S(1)} %get-tuple-element.9.x_sum, ...), custom_call_target="tpu_custom_call" | custom-call | tf_op jit(solution)/shard_map/pallas_call | solution.py:212

commit v3 on v2

--- a/solution.py
+++ b/solution.py
@@ -11,6 +11,7 @@
 CHUNK = 128
 EPS = 1e-06
 MEBI = 2**20
+RING = 32
 
 
 def inverse_norm(wide):
@@ -42,7 +43,8 @@
 
 
 def exchange(n, scale_ref, bias_ref, image_ref, text_ref, x_raw, x_low, x_sum, y_grad, last, y_raw, y_low, y_sum,
-             passed, near, far, unit, load_sem, link_send, link_recv, pass_send, pass_recv, pair_send, pair_recv):
+             passed, near, far, unit, load_sem, link_send, link_recv, pass_send, pass_recv, pair_send, pair_recv,
+             help_send, go):
     rows, width = x_raw.shape
     parts = rows // CHUNK
     me = lax.axis_index("blk")
@@ -50,6 +52,12 @@
     partner = me + 1 - 2 * core
     ahead = lax.rem(me + 2 - 4 * core + n, n)
     behind = lax.rem(me - 2 + 4 * core + n, n)
+    chip = lax.rem(me // 2, RING)
+    place = chip + core * (RING - 1 - 2 * chip)
+    is_first = place == 0
+    giver = (core == 1) & (place == RING - 1)
+    helper = (core == 0) & is_first
+    helped = (2, 3)
 
     barrier = pltpu.get_barrier_semaphore()
     for other in (behind, partner):
@@ -75,20 +83,41 @@
     def link(src, i):
         return remote(src, far.at[part(i)], link_send.at[i], link_recv.at[i], ahead)
 
-    def hand(i):
-        return remote(x_raw.at[part(i)], passed.at[part(i)], pass_send.at[i], pass_recv.at[i], partner)
+    def hand(src, i):
+        return remote(src, passed.at[part(i)], pass_send.at[i], pass_recv.at[i], partner)
 
     def pair(src, i):
         return remote(src, near.at[part(i)], pair_send.at[i], pair_recv.at[i], partner)
 
+    def help_out(k):
+        i = 2 * parts + helped[k]
+        return remote(near.at[part(parts + 1 + helped[k])], far.at[part(i)], help_send.at[k], link_recv.at[i],
+                      lax.rem(me - 1 + n, n))
+
+    pl.semaphore_wait(barrier, 2)
+
+    def begin(x_ref, y_ref):
+        link(y_ref.at[part(0)], 0).start()
+        for i in range(parts):
+            hand(x_ref.at[part(i)], i).start()
+
+    pl.when(core == 0)(lambda: begin(image_ref, text_ref))
+    pl.when(core == 1)(lambda: begin(text_ref, image_ref))
+
     pltpu.make_async_copy(text_ref, y_raw, load_sem.at[0]).wait()
+    for i in range(parts):
+        pair(y_raw.at[part(i)], i).start()
+
+    @pl.when(giver)
+    def _():
+        pl.semaphore_signal(go, inc=1, device_id=(partner,), device_id_type=MESH)
+
+    def own():
+        for i in range(1, parts):
+            link(y_raw.at[part(i)], parts + i).start()
+
+    pl.when(is_first)(own)
     pltpu.make_async_copy(text_ref, x_raw, load_sem.at[1]).wait()
-    pl.semaphore_wait(barrier, 2)
-    link(y_raw.at[part(0)], 0).start()
-    for i in range(parts):
-        hand(i).start()
-    for i in range(parts):
-        pair(y_raw.at[part(i)], i).start()
 
     def lower(src, start, dst, count):
         @pl.loop(0, count)
@@ -104,10 +133,9 @@
 
     lower(x_raw, 0, x_low, parts)
     for i in range(parts):
-        hand(i).wait_recv()
+        hand(x_raw.at[part(i)], i).wait_recv()
         link(passed.at[part(i)], 1 + i).start()
-    for i in range(1, parts):
-        link(y_raw.at[part(i)], parts + i).start()
+    pl.when(jnp.logical_not(is_first))(own)
     lower(y_raw, 0, y_low, parts)
 
     x_sum[...] = jnp.dot(
@@ -122,7 +150,9 @@
         for i in range(block * parts, (block + 1) * parts):
             link(y_raw.at[part(0)], i).wait_recv()
             pair(far.at[part(i)], i + parts).start()
-            if 1 <= i <= parts:
+            if i - 1 in helped:
+                pl.when(jnp.logical_not(giver))(lambda: link(far.at[part(i)], i + 2 * parts - 1).start())
+            elif 1 <= i <= parts:
                 link(far.at[part(i)], i + 2 * parts - 1).start()
         meet(x_low, far, block * rows, x_sum)
         for i in range(block * parts, (block + 1) * parts):
@@ -134,18 +164,32 @@
         here = pl.ds(pl.multiple_of(i * CHUNK, CHUNK), CHUNK)
         y_grad[here, :] = norm_back(y_raw[here, :], y_sum[here, :])
 
+    @pl.when(helper)
+    def _():
+        pl.semaphore_wait(go, 1)
+        for k in range(len(helped)):
+            help_out(k).start()
+
     for i in range(2 * parts, 3 * parts - 1):
         link(y_raw.at[part(0)], i).wait_recv()
     meet(x_low, far, 2 * rows, x_sum, parts - 1)
 
     for i in range(parts):
-        hand(i).wait_send()
+        hand(x_raw.at[part(i)], i).wait_send()
     for i in range(3 * parts):
         pair(y_raw.at[part(0)], i).wait_send()
     for i in range(3 * parts):
-        link(y_raw.at[part(0)], i).wait_send()
+        if i - 2 * parts in helped:
+            pl.when(jnp.logical_not(giver))(lambda: link(y_raw.at[part(0)], i).wait_send())
+        else:
+            link(y_raw.at[part(0)], i).wait_send()
     link(y_raw.at[part(0)], 3 * parts - 1).wait_recv()
     last[...] = low(far[part(3 * parts - 1), :])
+
+    @pl.when(helper)
+    def _():
+        for k in range(len(helped)):
+            help_out(k).wait_send()
 
 
 def conclude(scale_ref, bias_ref, x_raw, x_low, x_sum, y_grad, last, image_out, text_out, x_grad, weights, store_sem):
@@ -203,6 +247,8 @@
                 dma((parts,)),
                 dma((3 * parts,)),
                 dma((3 * parts,)),
+                dma((2,)),
+                pltpu.SemaphoreType.REGULAR,
             ],
             compiler_params=pltpu.CompilerParams(
                 collective_id=0, has_side_effects=True, vmem_limit_bytes=40 * MEBI),

time: 55.7 us -> 54.7 us (0.982)
  Pallas kernels: 53.5 us -> 52.5 us
    pallas_call x1, Pallas kernels: 50.7 us -> 49.6 us  [local(): pl.pallas_call(functools.partial(exchange, n), out_shape=(half, half, wid...]
where the time goes in v3:
time: 54.7 us; the launch traced here: 54.6 us
  Pallas kernels  52.5 us (96%)
  between operations  2.09 us (4%)
    pallas_call x1, Pallas kernels, local(): pl.pallas_call(functools.partial(exchange, n), out_shape=(half, half, wid...  49.6 us
    pallas_call x1, Pallas kernels, local(): pl.pallas_call(conclude, out_shape=(out, out), in_specs=[in_smem] * 2 + [...  2.82 us

profile of v3, /device:TPU:0, one launch (start us, length us, event | category | flops | bytes accessed | tf_op | source)
XLA Modules:
  0.0 54.6 jit_solution(6595786824721498416)
XLA Ops:
  1.9 49.6 %shard_map.59 = (bf16[512,1152]{1,0:T(8,128)(2,1)S(1)}, bf16[512,1152]{1,0:T(8,128)(2,1)S(1)}, f32[512,1152]{1,0:T(8,128)S(1)}, f32[512,1152]{1,0:T(8,128)S(1)}, bf16[128,1152]{1,0:T(8,128)(2,1)S(1)}) custom-call(f32[1]{0:T(128)S(6)} %copy.6.scale_ref, f32[1]{0:T(128)S(6)} %copy.7.bias_ref, bf16[512,1152]{1,0:T(8,128)(2,1)} %image_ref.1, ...), custom_call_target="tpu_custom_call" | custom-call | tf_op jit(solution)/shard_map/pallas_call | solution.py:233
  51.6 2.8 %shard_map.60 = (f32[512,1152]{1,0:T(8,128)}, f32[512,1152]{1,0:T(8,128)}) custom-call(f32[1]{0:T(128)S(6)} %copy.6.scale_ref, f32[1]{0:T(128)S(6)} %copy.7.bias_ref, bf16[512,1152]{1,0:T(8,128)(2,1)S(1)} %get-tuple-element.7.x_raw, bf16[512,1152]{1,0:T(8,128)(2,1)S(1)} %get-tuple-element.8.x_low, f32[512,1152]{1,0:T(8,128)S(1)} %get-tuple-element.9.x_sum, ...), custom_call_target="tpu_custom_call" | custom-call | tf_op jit(solution)/shard_map/pallas_call | solution.py:258

commit v4 on v3

--- a/solution.py
+++ b/solution.py
@@ -9,6 +9,7 @@
 
 MESH = pl.DeviceIdType.MESH
 CHUNK = 128
+TILE = 128
 EPS = 1e-06
 MEBI = 2**20
 RING = 32
@@ -42,7 +43,8 @@
     return (wide * inverse_norm(wide)).astype(jnp.bfloat16)
 
 
-def exchange(n, scale_ref, bias_ref, image_ref, text_ref, x_raw, x_low, x_sum, y_grad, last, y_raw, y_low, y_sum,
+def exchange(n, scale_ref, bias_ref, image_ref, text_ref, x_low, x_unit, x_inverse, x_sum, y_grad, last, x_raw, y_raw,
+             y_low, y_sum,
              passed, near, far, unit, load_sem, link_send, link_recv, pass_send, pass_recv, pair_send, pair_recv,
              help_send, go):
     rows, width = x_raw.shape
@@ -57,7 +59,7 @@
     is_first = place == 0
     giver = (core == 1) & (place == RING - 1)
     helper = (core == 0) & is_first
-    helped = (2, 3)
+    helped = (3,)
 
     barrier = pltpu.get_barrier_semaphore()
     for other in (behind, partner):
@@ -163,6 +165,10 @@
     def _(i):
         here = pl.ds(pl.multiple_of(i * CHUNK, CHUNK), CHUNK)
         y_grad[here, :] = norm_back(y_raw[here, :], y_sum[here, :])
+        wide = x_raw[here, :].astype(jnp.float32)
+        inverse = inverse_norm(wide)
+        x_inverse[here, :] = inverse
+        x_unit[here, :] = wide * inverse
 
     @pl.when(helper)
     def _():
@@ -192,8 +198,8 @@
             help_out(k).wait_send()
 
 
-def conclude(scale_ref, bias_ref, x_raw, x_low, x_sum, y_grad, last, image_out, text_out, x_grad, weights, store_sem):
-    rows, _ = x_raw.shape
+def conclude(scale_ref, bias_ref, x_low, x_unit, x_inverse, x_sum, y_grad, last, image_out, text_out, x_grad, weights, store_sem):
+    rows, _ = x_low.shape
     parts = rows // CHUNK
     core = lax.rem(lax.axis_index("blk"), 2)
 
@@ -205,16 +211,21 @@
         pl.when(core == 0)(lambda: store(y_grad.at[here], text_out.at[here], parts + i).start())
         pl.when(core == 1)(lambda: store(y_grad.at[here], image_out.at[here], parts + i).start())
     weights[...] = weigh(x_low[...], last[...], scale_ref[0], bias_ref[0])
+    tiles = rows // TILE
+    for i in range(tiles):
+        here = pl.ds(i * TILE, TILE)
+        grad = x_sum[here, :] + jnp.dot(weights[here, :], last[...], preferred_element_type=jnp.float32)
+        own = x_unit[here, :]
+        inner = jnp.sum(own * grad, axis=-1, keepdims=True)
+        x_grad[here, :] = (grad - own * inner) * x_inverse[here, :]
+        pl.when(core == 0)(lambda: store(x_grad.at[here], image_out.at[here], 2 * parts + i).start())
+        pl.when(core == 1)(lambda: store(x_grad.at[here], text_out.at[here], 2 * parts + i).start())
     for i in range(parts):
         here = pl.ds(i * CHUNK, CHUNK)
-        grad = x_sum[here, :] + jnp.dot(weights[here, :], last[...], preferred_element_type=jnp.float32)
-        x_grad[here, :] = norm_back(x_raw[here, :], grad)
-        pl.when(core == 0)(lambda: store(x_grad.at[here], image_out.at[here], i).start())
-        pl.when(core == 1)(lambda: store(x_grad.at[here], text_out.at[here], i).start())
-    for i in range(parts):
-        here = pl.ds(i * CHUNK, CHUNK)
-        store(x_grad.at[here], image_out.at[here], i).wait()
         store(y_grad.at[here], text_out.at[here], parts + i).wait()
+    for i in range(tiles):
+        here = pl.ds(i * TILE, TILE)
+        store(x_grad.at[here], image_out.at[here], 2 * parts + i).wait()
 
 
 def solution(mesh):
@@ -232,11 +243,11 @@
         in_smem = pl.BlockSpec(memory_space=pltpu.SMEM)
         held = pl.pallas_call(
             functools.partial(exchange, n),
-            out_shape=(half, half, wide, wide, piece),
+            out_shape=(half, wide, pltpu.VMEM((rows, 1), jnp.float32), wide, wide, piece),
             in_specs=[in_smem] * 2 + [in_hbm] * 2,
-            out_specs=(in_vmem,) * 5,
+            out_specs=(in_vmem,) * 6,
             scratch_shapes=[
-                half, half, wide, half,
+                half, half, half, wide, half,
                 pltpu.VMEM((3 * rows, width), jnp.bfloat16),
                 pltpu.VMEM((3 * rows, width), jnp.bfloat16),
                 half,
@@ -247,7 +258,7 @@
                 dma((parts,)),
                 dma((3 * parts,)),
                 dma((3 * parts,)),
-                dma((2,)),
+                dma((1,)),
                 pltpu.SemaphoreType.REGULAR,
             ],
             compiler_params=pltpu.CompilerParams(
@@ -258,9 +269,9 @@
         return pl.pallas_call(
             conclude,
             out_shape=(out, out),
-            in_specs=[in_smem] * 2 + [in_vmem] * 5,
+            in_specs=[in_smem] * 2 + [in_vmem] * 6,
             out_specs=(in_hbm,) * 2,
-            scratch_shapes=[wide, pltpu.VMEM((rows, CHUNK), jnp.bfloat16), dma((2 * parts,))],
+            scratch_shapes=[wide, pltpu.VMEM((rows, CHUNK), jnp.bfloat16), dma((2 * parts + rows // TILE,))],
             compiler_params=pltpu.CompilerParams(vmem_limit_bytes=16 * MEBI),
         )(scale, bias, *held)
 

time: 54.7 us -> 54.1 us (0.989)
  Pallas kernels: 52.5 us -> 51.9 us
where the time goes in v4:
time: 54.1 us; the launch traced here: 54 us
  Pallas kernels  51.9 us (96%)
  between operations  2.09 us (4%)
    pallas_call x1, Pallas kernels, local(): pl.pallas_call(functools.partial(exchange, n), out_shape=(half, wide, plt...  49.4 us
    pallas_call x1, Pallas kernels, local(): pl.pallas_call(conclude, out_shape=(out, out), in_specs=[in_smem] * 2 + [...  2.55 us

profile of v4, /device:TPU:0, one launch (start us, length us, event | category | flops | bytes accessed | tf_op | source)
XLA Modules:
  0.0 54.0 jit_solution(9134565886453399818)
XLA Ops:
  1.9 49.4 %shard_map.59 = (bf16[512,1152]{1,0:T(8,128)(2,1)S(1)}, f32[512,1152]{1,0:T(8,128)S(1)}, f32[512,1]{1,0:T(8,128)S(1)}, f32[512,1152]{1,0:T(8,128)S(1)}, f32[512,...) custom-call(f32[1]{0:T(128)S(6)} %copy.6.scale_ref, f32[1]{0:T(128)S(6)} %copy.7.bias_ref, bf16[512,1152]{1,0:T(8,128)(2,1)} %image_ref.1, ...), custom_call_target="tpu_custom_call" | custom-call | tf_op jit(solution)/shard_map/pallas_call | solution.py:244
  51.3 2.5 %shard_map.60 = (f32[512,1152]{1,0:T(8,128)}, f32[512,1152]{1,0:T(8,128)}) custom-call(f32[1]{0:T(128)S(6)} %copy.6.scale_ref, f32[1]{0:T(128)S(6)} %copy.7.bias_ref, bf16[512,1152]{1,0:T(8,128)(2,1)S(1)} %get-tuple-element.8.x_low, f32[512,1152]{1,0:T(8,128)S(1)} %get-tuple-element.9.x_unit, f32[512,1]{1,0:T(8,128)S(1)} %get-tuple-element.10.x_inverse, ...), custom_call_target="tpu_custom_call" | custom-call | tf_op jit(solution)/shard_map/pallas_call | solution.py:269

commit v5 on v4

--- a/solution.py
+++ b/solution.py
@@ -9,7 +9,6 @@
 
 MESH = pl.DeviceIdType.MESH
 CHUNK = 128
-TILE = 128
 EPS = 1e-06
 MEBI = 2**20
 RING = 32
@@ -65,13 +64,6 @@
     for other in (behind, partner):
         pl.semaphore_signal(barrier, inc=1, device_id=(other,), device_id_type=MESH)
 
-    def load(x_ref, y_ref):
-        pltpu.make_async_copy(y_ref, y_raw, load_sem.at[0]).start()
-        pltpu.make_async_copy(x_ref, x_raw, load_sem.at[1]).start()
-
-    pl.when(core == 0)(lambda: load(image_ref, text_ref))
-    pl.when(core == 1)(lambda: load(text_ref, image_ref))
-
     factor = scale_ref[0]
     offset = bias_ref[0]
 
@@ -102,6 +94,8 @@
         link(y_ref.at[part(0)], 0).start()
         for i in range(parts):
             hand(x_ref.at[part(i)], i).start()
+        pltpu.make_async_copy(y_ref, y_raw, load_sem.at[0]).start()
+        pltpu.make_async_copy(x_ref, x_raw, load_sem.at[1]).start()
 
     pl.when(core == 0)(lambda: begin(image_ref, text_ref))
     pl.when(core == 1)(lambda: begin(text_ref, image_ref))
@@ -206,26 +200,25 @@
     def store(src, out, i):
         return pltpu.make_async_copy(src, out, store_sem.at[i])
 
-    for i in range(parts):
-        here = pl.ds(i * CHUNK, CHUNK)
-        pl.when(core == 0)(lambda: store(y_grad.at[here], text_out.at[here], parts + i).start())
-        pl.when(core == 1)(lambda: store(y_grad.at[here], image_out.at[here], parts + i).start())
-    weights[...] = weigh(x_low[...], last[...], scale_ref[0], bias_ref[0])
-    tiles = rows // TILE
-    for i in range(tiles):
-        here = pl.ds(i * TILE, TILE)
-        grad = x_sum[here, :] + jnp.dot(weights[here, :], last[...], preferred_element_type=jnp.float32)
-        own = x_unit[here, :]
-        inner = jnp.sum(own * grad, axis=-1, keepdims=True)
-        x_grad[here, :] = (grad - own * inner) * x_inverse[here, :]
-        pl.when(core == 0)(lambda: store(x_grad.at[here], image_out.at[here], 2 * parts + i).start())
-        pl.when(core == 1)(lambda: store(x_grad.at[here], text_out.at[here], 2 * parts + i).start())
-    for i in range(parts):
-        here = pl.ds(i * CHUNK, CHUNK)
-        store(y_grad.at[here], text_out.at[here], parts + i).wait()
-    for i in range(tiles):
-        here = pl.ds(i * TILE, TILE)
-        store(x_grad.at[here], image_out.at[here], 2 * parts + i).wait()
+    def run(x_out, y_out):
+        for i in range(parts):
+            here = pl.ds(i * CHUNK, CHUNK)
+            store(y_grad.at[here], y_out.at[here], parts + i).start()
+        weights[...] = weigh(x_low[...], last[...], scale_ref[0], bias_ref[0])
+        for i in range(parts):
+            here = pl.ds(i * CHUNK, CHUNK)
+            grad = x_sum[here, :] + jnp.dot(weights[here, :], last[...], preferred_element_type=jnp.float32)
+            own = x_unit[here, :]
+            inner = jnp.sum(own * grad, axis=-1, keepdims=True)
+            x_grad[here, :] = (grad - own * inner) * x_inverse[here, :]
+            store(x_grad.at[here], x_out.at[here], i).start()
+        for i in range(parts):
+            here = pl.ds(i * CHUNK, CHUNK)
+            store(y_grad.at[here], y_out.at[here], parts + i).wait()
+            store(x_grad.at[here], x_out.at[here], i).wait()
+
+    pl.when(core == 0)(lambda: run(image_out, text_out))
+    pl.when(core == 1)(lambda: run(text_out, image_out))
 
 
 def solution(mesh):
@@ -271,7 +264,7 @@
             out_shape=(out, out),
             in_specs=[in_smem] * 2 + [in_vmem] * 6,
             out_specs=(in_hbm,) * 2,
-            scratch_shapes=[wide, pltpu.VMEM((rows, CHUNK), jnp.bfloat16), dma((2 * parts + rows // TILE,))],
+            scratch_shapes=[wide, pltpu.VMEM((rows, CHUNK), jnp.bfloat16), dma((2 * parts,))],
             compiler_params=pltpu.CompilerParams(vmem_limit_bytes=16 * MEBI),
         )(scale, bias, *held)
 

time: 54.1 us -> 53.9 us (level)
  no operation moved by 1% of the time
where the time goes in v5:
time: 53.9 us; the launch traced here: 53.8 us
  Pallas kernels  51.9 us (96%)
  between operations  1.93 us (4%)
    pallas_call x1, Pallas kernels, local(): pl.pallas_call(functools.partial(exchange, n), out_shape=(half, wide, plt...  49.3 us
    pallas_call x1, Pallas kernels, local(): pl.pallas_call(conclude, out_shape=(out, out), in_specs=[in_smem] * 2 + [...  2.57 us

profile of v5, /device:TPU:0, one launch (start us, length us, event | category | flops | bytes accessed | tf_op | source)
XLA Modules:
  0.0 53.8 jit_solution(5627770640208123949)
XLA Ops:
  1.9 49.3 %shard_map.59 = (bf16[512,1152]{1,0:T(8,128)(2,1)S(1)}, f32[512,1152]{1,0:T(8,128)S(1)}, f32[512,1]{1,0:T(8,128)S(1)}, f32[512,1152]{1,0:T(8,128)S(1)}, f32[512,...) custom-call(f32[1]{0:T(128)S(6)} %copy.6.scale_ref, f32[1]{0:T(128)S(6)} %copy.7.bias_ref, bf16[512,1152]{1,0:T(8,128)(2,1)} %image_ref.1, ...), custom_call_target="tpu_custom_call" | custom-call | tf_op jit(solution)/shard_map/pallas_call | solution.py:237
  51.2 2.6 %shard_map.60 = (f32[512,1152]{1,0:T(8,128)}, f32[512,1152]{1,0:T(8,128)}) custom-call(f32[1]{0:T(128)S(6)} %copy.6.scale_ref, f32[1]{0:T(128)S(6)} %copy.7.bias_ref, bf16[512,1152]{1,0:T(8,128)(2,1)S(1)} %get-tuple-element.8.x_low, f32[512,1152]{1,0:T(8,128)S(1)} %get-tuple-element.9.x_unit, f32[512,1]{1,0:T(8,128)S(1)} %get-tuple-element.10.x_inverse, ...), custom_call_target="tpu_custom_call" | custom-call | tf_op jit(solution)/shard_map/pallas_call | solution.py:262

commit v6 on v5

--- a/solution.py
+++ b/solution.py
@@ -201,9 +201,7 @@
         return pltpu.make_async_copy(src, out, store_sem.at[i])
 
     def run(x_out, y_out):
-        for i in range(parts):
-            here = pl.ds(i * CHUNK, CHUNK)
-            store(y_grad.at[here], y_out.at[here], parts + i).start()
+        store(y_grad, y_out, parts).start()
         weights[...] = weigh(x_low[...], last[...], scale_ref[0], bias_ref[0])
         for i in range(parts):
             here = pl.ds(i * CHUNK, CHUNK)
@@ -214,8 +212,8 @@
             store(x_grad.at[here], x_out.at[here], i).start()
         for i in range(parts):
             here = pl.ds(i * CHUNK, CHUNK)
-            store(y_grad.at[here], y_out.at[here], parts + i).wait()
             store(x_grad.at[here], x_out.at[here], i).wait()
+        store(y_grad, y_out, parts).wait()
 
     pl.when(core == 0)(lambda: run(image_out, text_out))
     pl.when(core == 1)(lambda: run(text_out, image_out))
@@ -264,7 +262,7 @@
             out_shape=(out, out),
             in_specs=[in_smem] * 2 + [in_vmem] * 6,
             out_specs=(in_hbm,) * 2,
-            scratch_shapes=[wide, pltpu.VMEM((rows, CHUNK), jnp.bfloat16), dma((2 * parts,))],
+            scratch_shapes=[wide, pltpu.VMEM((rows, CHUNK), jnp.bfloat16), dma((parts + 1,))],
             compiler_params=pltpu.CompilerParams(vmem_limit_bytes=16 * MEBI),
         )(scale, bias, *held)
 

time: 53.9 us -> 53.9 us (level)
  no operation moved by 1% of the time
where the time goes in v6:
time: 53.9 us; the launch traced here: 53.7 us
  Pallas kernels  51.8 us (96%)
  between operations  1.93 us (4%)
    pallas_call x1, Pallas kernels, local(): pl.pallas_call(functools.partial(exchange, n), out_shape=(half, wide, plt...  49.3 us
    pallas_call x1, Pallas kernels, local(): pl.pallas_call(conclude, out_shape=(out, out), in_specs=[in_smem] * 2 + [...  2.5 us

profile of v6, /device:TPU:0, one launch (start us, length us, event | category | flops | bytes accessed | tf_op | source)
XLA Modules:
  0.0 53.7 jit_solution(2839845374324906217)
XLA Ops:
  1.9 49.3 %shard_map.59 = (bf16[512,1152]{1,0:T(8,128)(2,1)S(1)}, f32[512,1152]{1,0:T(8,128)S(1)}, f32[512,1]{1,0:T(8,128)S(1)}, f32[512,1152]{1,0:T(8,128)S(1)}, f32[512,...) custom-call(f32[1]{0:T(128)S(6)} %copy.6.scale_ref, f32[1]{0:T(128)S(6)} %copy.7.bias_ref, bf16[512,1152]{1,0:T(8,128)(2,1)} %image_ref.1, ...), custom_call_target="tpu_custom_call" | custom-call | tf_op jit(solution)/shard_map/pallas_call | solution.py:235
  51.2 2.5 %shard_map.60 = (f32[512,1152]{1,0:T(8,128)}, f32[512,1152]{1,0:T(8,128)}) custom-call(f32[1]{0:T(128)S(6)} %copy.6.scale_ref, f32[1]{0:T(128)S(6)} %copy.7.bias_ref, bf16[512,1152]{1,0:T(8,128)(2,1)S(1)} %get-tuple-element.8.x_low, f32[512,1152]{1,0:T(8,128)S(1)} %get-tuple-element.9.x_unit, f32[512,1]{1,0:T(8,128)S(1)} %get-tuple-element.10.x_inverse, ...), custom_call_target="tpu_custom_call" | custom-call | tf_op jit(solution)/shard_map/pallas_call | solution.py:260
